TPU v7x, 32 devices: a whole 2x2x4 slice. The times are simulated.
32 devices in a mesh: leaf: 16 (over z, y, x), vec: 2 (over core).
Axes of the slice: x: 2, y: 2, z: 4, core: 2. Of those that a mesh axis runs over, the one named last changes fastest.
Arguments:
- points: bfloat16 [3, 131072], P(None, 'leaf'), may hold values from -4 to 4
- vectors: bfloat16 [16, 131072], P('vec', 'leaf'), may hold values from -6 to 6
- leaf_order: int32 [16, 8192], P('leaf'), may hold values from 0 to 8191, each once within a row
- leaf_bases: bfloat16 [256, 64, 512], P('leaf'), may hold values from -0.25 to 0.25
- transfers: bfloat16 [480, 64, 64], P('leaf'), may hold values from -0.5 to 0.5
- coupling_blocks: bfloat16 [4096, 64, 64], P('leaf'), may hold values from -0.75 to 0.75
- block_source: int32 [4096], P('leaf'), may hold values from 0 to 30, as said below
- block_owner: int32 [4096, 1], P('leaf'), may hold values from 0 to 15; in each aligned block of 256 rows (0 to 255, 256 to 511, ...) at most 32 rows name the same one
- block_target: int32 [4096], P('leaf'), may hold values from 0 to 30, as said below
- up_transfer: bfloat16 [30, 64, 64], replicated, may hold values from -0.5 to 0.5
- up_coupling: bfloat16 [30, 64, 64], replicated, as said below
Outputs:
- product: bfloat16 [16, 131072], P('vec', 'leaf')
Inputs may be any that keep to these rules, and one draw needn't show every extreme that they name: `leaf_order`: within each row, each point of the device once. `block_source`: A cluster of the subtree of the device that stores the block, numbered leaves first and level by level up to the root. `block_target`: A cluster of the subtree of the device block_owner names, in the same numbering, on the same level as the block's source cluster. `block_owner`: of the 256 blocks stored on one device, at most 32 name the same device, and exactly 32 name some device; every device is named by some block. `up_coupling`: coupling matrices of sibling clusters of the upper tree, finite.
All inputs are finite; a program needn't handle non-finite values.
Results may differ from a plain program's by a relative error of at most 0.0065.
Values may be sent and summed in bfloat16 or wider, within the bound.
A program may use at most 128 MiB of HBM per device.

v0:
```python
import functools

import jax
import jax.numpy as jnp
from jax import lax
from jax.experimental import pallas as pl
from jax.experimental.pallas import tpu as pltpu
from jax.sharding import PartitionSpec as P

NEAR = 2
WIDTH = 256
SHIFT = 8
ROWS = 16
SLOTS = 32
near_scale = 8.0
smooth_sq = 0.0025
f32, bf16, i32 = jnp.float32, jnp.bfloat16, jnp.int32


def contract(left, right, dim_left, dim_right):
    return lax.dot_general(
        left, right, (((dim_left,), (dim_right,)), ((), ())), preferred_element_type=f32
    )


def nn(left, right):
    return contract(left, right, 1, 0)


def nt(left, right):
    return contract(left, right, 1, 1)


def tn(left, right):
    return contract(left, right, 0, 0)


def two_parts(value):
    high = value.astype(bf16).astype(f32)
    return jnp.concatenate([high, value - high], axis=0).astype(bf16)


def wide(product, value, matrix):
    count = value.shape[0]
    both = product(two_parts(value), matrix)
    return both[:count] + both[count:]


def one_hot(rows, index):
    ids = lax.broadcasted_iota(i32, (rows, index.shape[1]), 0)
    return jnp.where(ids == index, 1.0, 0.0).astype(bf16)


def twice(value):
    return jnp.concatenate([value, value], axis=1)


def leaf_columns(leaf, leaf_len):
    return pl.ds(pl.multiple_of(leaf * leaf_len, leaf_len), leaf_len)


def to_tree(vec_ref, pts_ref, perm_ref, bases_ref, tree_ref, tree_base, both, stack, coeff):
    local, cols = vec_ref.shape
    leaf_dev, rank, leaf_len = bases_ref.shape
    groups = cols // WIDTH
    both[...] = jnp.zeros_like(both)
    both[0:local] = vec_ref[...].astype(f32)
    both[8:11] = pts_ref[...].astype(f32)
    for group in range(groups):
        stack[group * ROWS : (group + 1) * ROWS, :] = both[
            :, group * WIDTH : (group + 1) * WIDTH
        ].astype(bf16)

    def one_leaf(leaf, carry):
        perm = perm_ref[:, leaf_columns(leaf, leaf_len)]
        high = lax.shift_right_logical(perm, SHIFT)
        picked = nn(stack[...], one_hot(WIDTH, perm & (WIDTH - 1)))
        total = jnp.where(high == 0, picked[:ROWS], 0.0)
        for group in range(1, groups):
            total = total + jnp.where(
                high == group, picked[group * ROWS : (group + 1) * ROWS], 0.0
            )
        tree = total.astype(bf16)
        tree_ref[:, leaf_columns(leaf + tree_base, leaf_len)] = tree
        own = nt(tree, bases_ref[leaf])[:local]
        coeff[pl.ds(pl.multiple_of(leaf * 8, 8), 8), :] = twice(own)
        return carry

    lax.fori_loop(0, leaf_dev, one_leaf, 0, unroll=4)


def climb(leaf_dev, rank, trans_ref, coeff):
    clusters = 2 * leaf_dev - 1
    coeff[clusters * 8 :, :] = jnp.zeros((coeff.shape[0] - clusters * 8, 2 * rank), f32)
    offset, number = 0, leaf_dev
    while number > 1:
        for parent in range(number // 2):
            total = 0.0
            for child in (offset + 2 * parent, offset + 2 * parent + 1):
                value = coeff[child * 8 : child * 8 + 8, :rank]
                total = total + wide(nn, value, trans_ref[child])
            place = (offset + number + parent) * 8
            coeff[place : place + 8, :] = twice(total)
        offset += number
        number //= 2


def couple(peers, blocks_ref, src_ref, dest, coeff, picked, made, send_ref):
    rank, _, blocks = blocks_ref.shape
    hot = one_hot(SLOTS, src_ref[...])
    for vec in range(8):
        values = coeff[pl.ds(vec, SLOTS, stride=8), :].astype(bf16)
        picked[vec * rank : (vec + 1) * rank, :] = tn(values, hot)[:rank]

    def part(block, carry):
        rows = pl.ds(pl.multiple_of(block * 16, 16), 16)

        def eight(step, sums):
            for inner in range(8):
                place = step * 8 + inner
                matrix = blocks_ref[place, rows, :].astype(f32)
                sums = tuple(
                    value + matrix * picked[pl.ds(vec * rank + place, 1), :]
                    for vec, value in enumerate(sums)
                )
            return sums

        zero = jnp.zeros((16, blocks), f32)
        sums = lax.fori_loop(0, rank // 8, eight, (zero,) * 8)
        for vec in range(8):
            place = pl.multiple_of(vec * rank + block * 16, 16)
            made[pl.ds(place, 16), :] = sums[vec].astype(bf16)
        return carry

    lax.fori_loop(0, rank // 16, part, 0)
    step_rows = 16 * SLOTS

    def some(step, carry):
        start = pl.multiple_of(step * step_rows, step_rows)
        send_ref[pl.ds(start, step_rows), :] = nt(
            one_hot(step_rows, dest - start), made[...]
        ).astype(bf16)
        return carry

    lax.fori_loop(0, peers * SLOTS // step_rows, some, 0)


def upper(peers, rank, ups, up_t, up_c):
    offset, number = 0, peers
    device = lax.axis_index("leaf")

    def at(node):
        return pl.ds(pl.multiple_of(node * 8, 8), 8)

    gains = []
    while number > 1:
        node = device // (peers // number)
        sibling = node + 1 - 2 * (node % 2)
        partner = ups[at(offset + sibling), :rank]
        gains.append((offset + node, wide(nn, partner, up_c[offset + node])))
        if number > 2:

            def pair(parent, carry, offset=offset, number=number):
                total = 0.0
                for side in range(2):
                    child = offset + 2 * parent + side
                    total = total + wide(nn, ups[at(child), :rank], up_t[child])
                ups[at(offset + number + parent), :] = twice(total)
                return carry

            lax.fori_loop(0, number // 2, pair, 0, unroll=min(8, number // 2))
        offset += number
        number //= 2
    top = gains[-1][1]
    for node, gain in reversed(gains[:-1]):
        top = wide(nt, top, up_t[node]) + gain
    return top


def near_features(mine, other, vx, fa, fb, cols):
    mine = mine.astype(f32)
    other = other.astype(f32)
    vx[:, cols] = jnp.concatenate([mine[:8], other[:8]], axis=0).astype(bf16)
    place = mine[8:]
    square = place[0:1] * place[0:1] + place[1:2] * place[1:2]
    square = square + place[2:3] * place[2:3] + smooth_sq / 2
    high = square.astype(bf16).astype(f32)
    middle = (square - high).astype(bf16).astype(f32)
    low = square - high - middle
    row = lax.broadcasted_iota(i32, place.shape, 0)
    one = jnp.ones_like(place)
    first = jnp.where(row == 3, high, jnp.where(row == 4, middle, jnp.where(row == 5, low, one)))
    first = jnp.where(row < 3, -2.0 * place, first)
    second = jnp.where(row < 6, one, jnp.where(row == 6, high, middle))
    second = jnp.where(row < 3, place, second)
    last = row == 0
    fa[:, cols] = jnp.concatenate([first, jnp.where(last, one, 0.0)], axis=0).astype(bf16)
    fb[:, cols] = jnp.concatenate([second, jnp.where(last, low, 0.0)], axis=0).astype(bf16)


def near_pairs(ext, fa, fb, acc, leaf_len, source, targets, back):
    src = leaf_columns(source, leaf_len)
    for target in targets:
        tgt = leaf_columns(target, leaf_len)
        kernel = lax.rsqrt(tn(fa[:, src], fb[:, tgt])).astype(bf16)
        acc[:, tgt] += nn(ext[:, src], kernel)
        if back and target is not source:
            acc[:, src] += nt(ext[:, tgt], kernel)


def finish(
    top_value, sums, near_all, trans_ref, bases_ref, perm_ref, out_ref, coupled, down, total
):
    leaf_dev, rank, leaf_len = bases_ref.shape
    cols = perm_ref.shape[1]
    groups = cols // WIDTH
    for vec in range(8):
        coupled[pl.ds(vec, SLOTS, stride=8), :] = twice(sums[:, vec * rank : (vec + 1) * rank])
    top = (2 * leaf_dev - 2) * 8
    down[top : top + 8, :] = top_value + coupled[top : top + 8, :rank]
    number = 1
    while number < leaf_dev:
        above = 2 * leaf_dev - 2 * number
        number *= 2
        offset = 2 * leaf_dev - 2 * number
        for child in range(number):
            parent = (above + child // 2) * 8
            place = (offset + child) * 8
            down[place : place + 8, :] = (
                wide(nt, down[parent : parent + 8, :], trans_ref[offset + child])
                + coupled[place : place + 8, :rank]
            )
    total[...] = jnp.zeros_like(total)

    def one_leaf(leaf, carry):
        here = leaf_columns(leaf, leaf_len)
        perm = perm_ref[:, here]
        high = lax.shift_right_logical(perm, SHIFT)
        value = down[pl.ds(pl.multiple_of(leaf * 8, 8), 8), :].astype(bf16)
        tree = nn(value, bases_ref[leaf]) + near_all[:, here] * (near_scale / leaf_len)
        tree = tree.astype(bf16).astype(f32)
        masked = jnp.concatenate(
            [jnp.where(high == group, tree, 0.0) for group in range(groups)], axis=0
        ).astype(bf16)
        total[...] += nt(masked, one_hot(WIDTH, perm & (WIDTH - 1)))
        return carry

    lax.fori_loop(0, leaf_dev, one_leaf, 0, unroll=4)
    for group in range(groups):
        out_ref[:, group * WIDTH : (group + 1) * WIDTH] = total[
            group * 8 : (group + 1) * 8, :
        ].astype(bf16)


def remote(source, target, send_sem, recv_sem, leaf, vec):
    return pltpu.make_async_remote_copy(
        src_ref=source,
        dst_ref=target,
        send_sem=send_sem,
        recv_sem=recv_sem,
        device_id=(leaf, vec),
        device_id_type=pl.DeviceIdType.MESH,
    )


def whole_kernel(
    peers, leaf_len, vec_any, pts_any, perm_any, src_any, owner_any, target_any,
    bases_any, trans_any, blocks_any, up_t_any, up_c_any, out_ref,
    vec_ref, pts_ref, perm_ref, src_ref, owner_ref, target_ref, bases, trans, blocks, up_t, up_c, both, stack, coeff, picked, made, send, recv, roots, ups,
    mine, other, halo, vx, fa, fb, acc, near_all, coupled, down, total,
    local_sem, part_sem, halo_send, halo_recv, root_send, root_recv, block_send, block_recv,
):
    cols = vec_any.shape[1]
    leaf_dev = cols // leaf_len
    rank = trans_any.shape[1]
    reach = NEAR * leaf_len
    half = leaf_dev // 2
    device = lax.axis_index("leaf")
    core = lax.axis_index("vec")
    partner = 1 - core
    cross = device - 1 + 2 * core
    has_cross = jnp.logical_and(cross >= 0, cross < peers)
    barrier = pltpu.get_barrier_semaphore()

    def greet(leaf, vec):
        pl.semaphore_signal(
            barrier, inc=1, device_id=(leaf, vec), device_id_type=pl.DeviceIdType.MESH
        )

    def each_peer(work):
        def body(step, carry):
            work(lax.rem(device + step, peers))
            return carry

        lax.fori_loop(1, peers, body, 0)

    each_peer(lambda peer: greet(peer, core))
    greet(device, partner)

    @pl.when(has_cross)
    def _():
        greet(cross, partner)

    loads = [
        pltpu.make_async_copy(source, target, local_sem.at[place])
        for place, (source, target) in enumerate(
            [(perm_any, perm_ref), (vec_any, vec_ref), (pts_any, pts_ref), (bases_any, bases),
             (trans_any, trans), (src_any, src_ref), (blocks_any, blocks),
             (owner_any, owner_ref), (target_any, target_ref), (up_t_any, up_t),
             (up_c_any, up_c)]
        )
    ]
    for load in loads:
        load.start()
    for load in loads[:4]:
        load.wait()
    to_tree(vec_ref, pts_ref, perm_ref, bases, mine, 0, both, stack, coeff)
    pl.semaphore_wait(barrier, peers + jnp.where(has_cross, 1, 0))

    seen = (half + NEAR) * leaf_len
    shift = (half - NEAR) * leaf_len
    to_partner = remote(
        mine.at[:, pl.ds(pl.multiple_of(partner * shift, 128), seen)], other,
        part_sem.at[0], part_sem.at[1], device, partner,
    )
    to_partner.start()
    to_right = remote(
        mine.at[:, cols - reach :], halo.at[core], halo_send.at[0], halo_recv.at[core],
        device + 1, 0,
    )
    to_left = remote(
        mine.at[:, :reach], halo.at[core], halo_send.at[1], halo_recv.at[core], device - 1, 1
    )
    not_last = device < peers - 1
    not_first = device > 0

    @pl.when(not_last)
    def _():
        to_right.start()

    @pl.when(not_first)
    def _():
        to_left.start()

    loads[4].wait()
    climb(leaf_dev, rank, trans, coeff)
    top = (2 * leaf_dev - 2) * 8
    mine_rows = pl.ds(pl.multiple_of(device * 8, 8), 8)
    ups[mine_rows, :] = coeff[top : top + 8, :]

    def root_copy(peer, place):
        return remote(
            coeff.at[top : top + 8, :], roots.at[place], root_send.at[peer],
            root_recv.at[place], peer, core,
        )

    each_peer(lambda peer: root_copy(peer, device).start())
    for load in loads[5:9]:
        load.wait()
    dest = owner_ref[...] * SLOTS + target_ref[...]
    couple(peers, blocks, src_ref, dest, coeff, picked, made, send)

    def slot(place):
        return pl.ds(pl.multiple_of(place * SLOTS, SLOTS), SLOTS)

    def block_copy(peer, place):
        return remote(
            send.at[slot(peer), :], recv.at[slot(place), :], block_send.at[peer],
            block_recv.at[place], peer, core,
        )

    each_peer(lambda peer: block_copy(peer, device).start())

    to_partner.wait_recv()
    off = NEAR * (1 - core)

    def features(place, carry):
        here = leaf_columns(place, leaf_len)
        there = leaf_columns(place + core * (half - NEAR), leaf_len)
        near_features(
            mine[:, there], other[:, here], vx, fa, fb, leaf_columns(place + off, leaf_len)
        )
        return carry

    lax.fori_loop(0, half + NEAR, features, 0)

    @pl.when(has_cross)
    def _():
        for vec in range(2):
            remote(
                mine.at[:, :reach], halo.at[vec], halo_send.at[vec], halo_recv.at[vec],
                device, partner,
            ).wait_recv()

    @pl.when(jnp.logical_not(has_cross))
    def _():
        halo[...] = jnp.zeros_like(halo)

    for place in range(NEAR):
        here = slice(place * leaf_len, (place + 1) * leaf_len)
        near_features(
            halo[core, :, here], halo[partner, :, here], vx, fa, fb,
            leaf_columns(place + core * (half + NEAR), leaf_len),
        )
    acc[...] = jnp.zeros_like(acc)
    near_pairs(vx, fa, fb, acc, leaf_len, 0, (2,), False)
    near_pairs(vx, fa, fb, acc, leaf_len, 1, (2, 3), False)

    def body(leaf, carry):
        near_pairs(vx, fa, fb, acc, leaf_len, leaf, (leaf, leaf + 1, leaf + 2), True)
        return carry

    lax.fori_loop(NEAR, half + NEAR, body, 0)
    part = half * leaf_len
    computed = pl.ds(pl.multiple_of(core * part, 128), part)
    to_near = remote(
        acc.at[8:16, pl.ds(reach, part)], near_all.at[:, computed],
        part_sem.at[2], part_sem.at[3], device, partner,
    )
    to_near.start()
    near_all[:, computed] = acc[:8, reach : reach + part]

    loads[9].wait()
    loads[10].wait()

    def root_in(peer):
        root_copy(peer, peer).wait_recv()
        ups[pl.ds(pl.multiple_of(peer * 8, 8), 8), :] = roots[peer]

    each_peer(root_in)
    top_value = upper(peers, rank, ups, up_t, up_c)

    def add(step, value):
        peer = lax.rem(device + step, peers)
        block_copy(peer, peer).wait_recv()
        return value + recv[slot(peer), :].astype(f32)

    sums = lax.fori_loop(1, peers, add, send[slot(device), :].astype(f32))
    to_near.wait_recv()
    finish(top_value, sums, near_all, trans, bases, perm_ref, out_ref, coupled, down, total)

    to_partner.wait_send()
    to_near.wait_send()

    @pl.when(not_last)
    def _():
        to_right.wait_send()

    @pl.when(not_first)
    def _():
        to_left.wait_send()

    def sent(peer):
        root_copy(peer, device).wait_send()
        block_copy(peer, device).wait_send()

    each_peer(sent)


def shards(
    points, vectors, leaf_order, leaf_bases, transfers, coupling_blocks,
    block_source, block_owner, block_target, up_transfer, up_coupling,
):
    peers = lax.axis_size("leaf")
    leaf_dev, rank, leaf_len = leaf_bases.shape
    cols = vectors.shape[1]
    blocks = coupling_blocks.shape[0]
    reach = NEAR * leaf_len
    groups = cols // WIDTH
    half = leaf_dev // 2
    span = (half + 2 * NEAR) * leaf_len
    by_block = jnp.transpose(coupling_blocks, (1, 2, 0))
    vmem = pl.BlockSpec(memory_space=pltpu.VMEM)
    anywhere = pl.BlockSpec(memory_space=pl.ANY)
    dma = pltpu.SemaphoreType.DMA
    return pl.pallas_call(
        functools.partial(whole_kernel, peers, leaf_len),
        out_shape=jax.ShapeDtypeStruct((8, cols), bf16),
        in_specs=[anywhere] * 11,
        out_specs=vmem,
        scratch_shapes=[
            pltpu.VMEM(vectors.shape, bf16),
            pltpu.VMEM(points.shape, bf16),
            pltpu.VMEM(leaf_order.shape, i32),
            pltpu.VMEM((1, blocks), i32),
            pltpu.VMEM((1, blocks), i32),
            pltpu.VMEM((1, blocks), i32),
            pltpu.VMEM(leaf_bases.shape, bf16),
            pltpu.VMEM(transfers.shape, bf16),
            pltpu.VMEM(by_block.shape, bf16),
            pltpu.VMEM(up_transfer.shape, bf16),
            pltpu.VMEM(up_coupling.shape, bf16),
            pltpu.VMEM((ROWS, cols), f32),
            pltpu.VMEM((groups * ROWS, WIDTH), bf16),
            pltpu.VMEM((SLOTS * 8, 2 * rank), f32),
            pltpu.VMEM((8 * rank, blocks), f32),
            pltpu.VMEM((8 * rank, blocks), bf16),
            pltpu.VMEM((peers * SLOTS, 8 * rank), bf16),
            pltpu.VMEM((peers * SLOTS, 8 * rank), bf16),
            pltpu.VMEM((peers, 8, 2 * rank), f32),
            pltpu.VMEM((2 * peers * 8, 2 * rank), f32),
            pltpu.VMEM((ROWS, cols), bf16),
            pltpu.VMEM((ROWS, (half + NEAR) * leaf_len), bf16),
            pltpu.VMEM((2, ROWS, reach), bf16),
            pltpu.VMEM((ROWS, span), bf16),
            pltpu.VMEM((ROWS, span), bf16),
            pltpu.VMEM((ROWS, span), bf16),
            pltpu.VMEM((ROWS, span), f32),
            pltpu.VMEM((8, cols), f32),
            pltpu.VMEM((SLOTS * 8, 2 * rank), f32),
            pltpu.VMEM((SLOTS * 8, rank), f32),
            pltpu.VMEM((groups * 8, WIDTH), f32),
            dma((11,)),
            dma((4,)),
            dma((2,)),
            dma((2,)),
            dma((peers,)),
            dma((peers,)),
            dma((peers,)),
            dma((peers,)),
        ],
        compiler_params=pltpu.CompilerParams(
            vmem_limit_bytes=64 * 1024 * 1024, collective_id=0, has_side_effects=True
        ),
        name="whole",
    )(
        vectors, points, leaf_order,
        block_source.reshape(1, blocks), block_owner.reshape(1, blocks),
        block_target.reshape(1, blocks),
        leaf_bases, transfers, by_block, up_transfer, up_coupling,
    )


def solution(mesh):
    return jax.shard_map(
        shards,
        mesh=mesh,
        in_specs=(
            P(None, "leaf"),
            P("vec", "leaf"),
            P("leaf", None),
            P("leaf", None, None),
            P("leaf", None, None),
            P("leaf", None, None),
            P("leaf"),
            P("leaf", None),
            P("leaf"),
            P(),
            P(),
        ),
        out_specs=P("vec", "leaf"),
        check_vma=False,
    )
```

profile of v0, /device:TPU:12, one launch (start us, length us, event | category | flops | bytes accessed | tf_op | source)
XLA Modules:
  0.0 34.0 jit_solution(1697688007776287392)
XLA Ops:
  0.0 32.4 %whole.1 = bf16[8,8192]{1,0:T(8,128)(2,1)} custom-call(bf16[8,8192]{1,0:T(8,128)(2,1)} %vec_any.1, bf16[3,8192]{1,0:T(4,128)(2,1)} %pts_any.1, s32[1,8192]{1,0:T(1,128)} %perm_any.1, s32[1,256]{1,0:T(1,128)} %bitcast.5, s32[1,256]{1,0:T(1,128)} %bitcast.6, s32[1,256]{1,0:T(1,128)} %bitcast.7, bf16[16,64,512]{2,1,0:T(8,128)(2,1)} %bases_any.1, ...), custom_call_target="tpu_custom_call" | custom-call | tf_op jit(solution)/shard_map/whole/pallas_call | solution.py:476
  32.4 1.6 %copy.13 = bf16[8,8192]{1,0:T(8,128)(2,1)} copy(bf16[8,8192]{1,0:T(8,128)(2,1)} %whole.1) | data formatting | bytes 262144
where the time goes:
time: 34.1 us; the launch traced here: 34 us
  Pallas kernels  32.4 us (95%)
  local copies, waits for them, and re-layouts  1.57 us (5%)
    pallas_call x1, Pallas kernels, shards(): pl.pallas_call(functools.partial(whole_kernel, peers, leaf_len), out_shap...  32.4 us
    unnamed x1, local copies, waits for them, and re-layouts  1.57 us

commit v1 on v0

--- a/solution.py
+++ b/solution.py
@@ -198,14 +198,22 @@
     fb[:, cols] = jnp.concatenate([second, jnp.where(last, low, 0.0)], axis=0).astype(bf16)
 
 
-def near_pairs(ext, fa, fb, acc, leaf_len, source, targets, back):
-    src = leaf_columns(source, leaf_len)
-    for target in targets:
-        tgt = leaf_columns(target, leaf_len)
-        kernel = lax.rsqrt(tn(fa[:, src], fb[:, tgt])).astype(bf16)
-        acc[:, tgt] += nn(ext[:, src], kernel)
-        if back and target is not source:
-            acc[:, src] += nt(ext[:, tgt], kernel)
+def near_leaf(vx, fa, fb, acc, leaf_len, leaf):
+    tgt = leaf_columns(leaf, leaf_len)
+    targets = fa[:, tgt]
+    total = None
+    for step in range(-NEAR, NEAR + 1):
+        src = leaf_columns(leaf + step, leaf_len)
+        kernel = lax.rsqrt(tn(targets, fb[:, src]).astype(bf16))
+        part = nt(kernel, vx[:, src])
+        total = part if total is None else total + part
+    unit = lax.broadcasted_iota(i32, (ROWS, ROWS), 0) == lax.broadcasted_iota(
+        i32, (ROWS, ROWS), 1
+    )
+    unit = jnp.where(unit, 1.0, 0.0).astype(bf16)
+    high = total.astype(bf16)
+    low = (total - high.astype(f32)).astype(bf16)
+    acc[:, tgt] = nt(unit, high) + nt(unit, low)
 
 
 def finish(
@@ -402,12 +410,9 @@
             halo[core, :, here], halo[partner, :, here], vx, fa, fb,
             leaf_columns(place + core * (half + NEAR), leaf_len),
         )
-    acc[...] = jnp.zeros_like(acc)
-    near_pairs(vx, fa, fb, acc, leaf_len, 0, (2,), False)
-    near_pairs(vx, fa, fb, acc, leaf_len, 1, (2, 3), False)
 
     def body(leaf, carry):
-        near_pairs(vx, fa, fb, acc, leaf_len, leaf, (leaf, leaf + 1, leaf + 2), True)
+        near_leaf(vx, fa, fb, acc, leaf_len, leaf)
         return carry
 
     lax.fori_loop(NEAR, half + NEAR, body, 0)

time: 34.1 us -> 38.5 us (1.13)
  Pallas kernels: 32.4 us -> 36.8 us
    pallas_call x1, Pallas kernels: 32.4 us -> 36.8 us  [shards(): pl.pallas_call(functools.partial(whole_kernel, peers, leaf_len), out_shap...]
where the time goes in v1:
time: 38.5 us; the launch traced here: 38.4 us
  Pallas kernels  36.8 us (96%)
  local copies, waits for them, and re-layouts  1.57 us (4%)
    pallas_call x1, Pallas kernels, shards(): pl.pallas_call(functools.partial(whole_kernel, peers, leaf_len), out_shap...  36.8 us
    unnamed x1, local copies, waits for them, and re-layouts  1.57 us

profile of v1, /device:TPU:12, one launch (start us, length us, event | category | flops | bytes accessed | tf_op | source)
XLA Modules:
  0.0 38.4 jit_solution(16260930308592352408)
XLA Ops:
  0.0 36.8 %whole.1 = bf16[8,8192]{1,0:T(8,128)(2,1)} custom-call(bf16[8,8192]{1,0:T(8,128)(2,1)} %vec_any.1, bf16[3,8192]{1,0:T(4,128)(2,1)} %pts_any.1, s32[1,8192]{1,0:T(1,128)} %perm_any.1, s32[1,256]{1,0:T(1,128)} %bitcast.5, s32[1,256]{1,0:T(1,128)} %bitcast.6, s32[1,256]{1,0:T(1,128)} %bitcast.7, bf16[16,64,512]{2,1,0:T(8,128)(2,1)} %bases_any.1, ...), custom_call_target="tpu_custom_call" | custom-call | tf_op jit(solution)/shard_map/whole/pallas_call | solution.py:481
  36.8 1.6 %copy.13 = bf16[8,8192]{1,0:T(8,128)(2,1)} copy(bf16[8,8192]{1,0:T(8,128)(2,1)} %whole.1) | data formatting | bytes 262144

commit v2 on v0

--- a/solution.py
+++ b/solution.py
@@ -74,13 +74,21 @@
     def one_leaf(leaf, carry):
         perm = perm_ref[:, leaf_columns(leaf, leaf_len)]
         high = lax.shift_right_logical(perm, SHIFT)
-        picked = nn(stack[...], one_hot(WIDTH, perm & (WIDTH - 1)))
-        total = jnp.where(high == 0, picked[:ROWS], 0.0)
-        for group in range(1, groups):
-            total = total + jnp.where(
-                high == group, picked[group * ROWS : (group + 1) * ROWS], 0.0
-            )
-        tree = total.astype(bf16)
+        parts = []
+        for part in range(leaf_len // WIDTH):
+            here = slice(part * WIDTH, (part + 1) * WIDTH)
+            high_part = high[:, here]
+            hot = one_hot(WIDTH, perm[:, here] & (WIDTH - 1))
+            total = None
+            for first in range(0, groups, ROWS):
+                picked = nn(stack[first * ROWS : (first + ROWS) * ROWS, :], hot)
+                for group in range(ROWS):
+                    chosen = jnp.where(
+                        high_part == first + group, picked[group * ROWS : (group + 1) * ROWS], 0.0
+                    )
+                    total = chosen if total is None else total + chosen
+            parts.append(total)
+        tree = jnp.concatenate(parts, axis=1).astype(bf16)
         tree_ref[:, leaf_columns(leaf + tree_base, leaf_len)] = tree
         own = nt(tree, bases_ref[leaf])[:local]
         coeff[pl.ds(pl.multiple_of(leaf * 8, 8), 8), :] = twice(own)
@@ -177,7 +185,7 @@
     return top
 
 
-def near_features(mine, other, vx, fa, fb, cols):
+def near_features(mine, other, vx, far, fb, cols):
     mine = mine.astype(f32)
     other = other.astype(f32)
     vx[:, cols] = jnp.concatenate([mine[:8], other[:8]], axis=0).astype(bf16)
@@ -194,18 +202,36 @@
     second = jnp.where(row < 6, one, jnp.where(row == 6, high, middle))
     second = jnp.where(row < 3, place, second)
     last = row == 0
-    fa[:, cols] = jnp.concatenate([first, jnp.where(last, one, 0.0)], axis=0).astype(bf16)
+    first = jnp.concatenate([first, jnp.where(last, one, 0.0)], axis=0).astype(bf16)
+    unit = lax.broadcasted_iota(i32, (ROWS, ROWS), 0)
+    unit = jnp.where(unit == lax.broadcasted_iota(i32, (ROWS, ROWS), 1), 1.0, 0.0).astype(bf16)
+    far[cols, :] = tn(first, unit).astype(bf16)
     fb[:, cols] = jnp.concatenate([second, jnp.where(last, low, 0.0)], axis=0).astype(bf16)
 
 
-def near_pairs(ext, fa, fb, acc, leaf_len, source, targets, back):
-    src = leaf_columns(source, leaf_len)
-    for target in targets:
-        tgt = leaf_columns(target, leaf_len)
-        kernel = lax.rsqrt(tn(fa[:, src], fb[:, tgt])).astype(bf16)
-        acc[:, tgt] += nn(ext[:, src], kernel)
-        if back and target is not source:
-            acc[:, src] += nt(ext[:, tgt], kernel)
+def near_source(vx, far, fb, acc, leaf_len, leaf, steps, back):
+    parts = leaf_len // WIDTH
+    sums = {}
+
+    def columns(step, part):
+        return pl.ds(pl.multiple_of((leaf + step) * leaf_len + part * WIDTH, WIDTH), WIDTH)
+
+    def add(key, value):
+        sums[key] = sums[key] + value if key in sums else value
+
+    for step in steps:
+        for tgt_part in range(parts):
+            for src_part in range(parts):
+                if step == 0 and src_part > tgt_part:
+                    continue
+                src, tgt = columns(0, src_part), columns(step, tgt_part)
+                square = nn(far[src, :], fb[:, tgt])
+                kernel = lax.rsqrt(square.astype(bf16))
+                add((step, tgt_part), nn(vx[:, src], kernel))
+                if back and (step, tgt_part) != (0, src_part):
+                    add((0, src_part), nt(vx[:, tgt], kernel))
+    for (step, part), value in sums.items():
+        acc[:, columns(step, part)] += value
 
 
 def finish(
@@ -267,7 +293,7 @@
     peers, leaf_len, vec_any, pts_any, perm_any, src_any, owner_any, target_any,
     bases_any, trans_any, blocks_any, up_t_any, up_c_any, out_ref,
     vec_ref, pts_ref, perm_ref, src_ref, owner_ref, target_ref, bases, trans, blocks, up_t, up_c, both, stack, coeff, picked, made, send, recv, roots, ups,
-    mine, other, halo, vx, fa, fb, acc, near_all, coupled, down, total,
+    mine, other, halo, vx, far, fb, acc, near_all, coupled, down, total,
     local_sem, part_sem, halo_send, halo_recv, root_send, root_recv, block_send, block_recv,
 ):
     cols = vec_any.shape[1]
@@ -378,11 +404,11 @@
         here = leaf_columns(place, leaf_len)
         there = leaf_columns(place + core * (half - NEAR), leaf_len)
         near_features(
-            mine[:, there], other[:, here], vx, fa, fb, leaf_columns(place + off, leaf_len)
+            mine[:, there], other[:, here], vx, far, fb, leaf_columns(place + off, leaf_len)
         )
         return carry
 
-    lax.fori_loop(0, half + NEAR, features, 0)
+    lax.fori_loop(0, half + NEAR, features, 0, unroll=2)
 
     @pl.when(has_cross)
     def _():
@@ -399,15 +425,15 @@
     for place in range(NEAR):
         here = slice(place * leaf_len, (place + 1) * leaf_len)
         near_features(
-            halo[core, :, here], halo[partner, :, here], vx, fa, fb,
+            halo[core, :, here], halo[partner, :, here], vx, far, fb,
             leaf_columns(place + core * (half + NEAR), leaf_len),
         )
     acc[...] = jnp.zeros_like(acc)
-    near_pairs(vx, fa, fb, acc, leaf_len, 0, (2,), False)
-    near_pairs(vx, fa, fb, acc, leaf_len, 1, (2, 3), False)
+    near_source(vx, far, fb, acc, leaf_len, 0, (2,), False)
+    near_source(vx, far, fb, acc, leaf_len, 1, (1, 2), False)
 
     def body(leaf, carry):
-        near_pairs(vx, fa, fb, acc, leaf_len, leaf, (leaf, leaf + 1, leaf + 2), True)
+        near_source(vx, far, fb, acc, leaf_len, leaf, (0, 1, 2), True)
         return carry
 
     lax.fori_loop(NEAR, half + NEAR, body, 0)
@@ -503,7 +529,7 @@
             pltpu.VMEM((ROWS, (half + NEAR) * leaf_len), bf16),
             pltpu.VMEM((2, ROWS, reach), bf16),
             pltpu.VMEM((ROWS, span), bf16),
-            pltpu.VMEM((ROWS, span), bf16),
+            pltpu.VMEM((span, ROWS), bf16),
             pltpu.VMEM((ROWS, span), bf16),
             pltpu.VMEM((ROWS, span), f32),
             pltpu.VMEM((8, cols), f32),

time: 34.1 us -> 41.3 us (1.21)
  Pallas kernels: 32.4 us -> 39.6 us
    pallas_call x1, Pallas kernels: 32.4 us -> 39.6 us  [shards(): pl.pallas_call(functools.partial(whole_kernel, peers, leaf_len), out_shap...]
where the time goes in v2:
time: 41.3 us; the launch traced here: 41.2 us
  Pallas kernels  39.6 us (96%)
  local copies, waits for them, and re-layouts  1.57 us (4%)
    pallas_call x1, Pallas kernels, shards(): pl.pallas_call(functools.partial(whole_kernel, peers, leaf_len), out_shap...  39.6 us
    unnamed x1, local copies, waits for them, and re-layouts  1.57 us

profile of v2, /device:TPU:12, one launch (start us, length us, event | category | flops | bytes accessed | tf_op | source)
XLA Modules:
  0.0 41.2 jit_solution(15778852722072739974)
XLA Ops:
  0.0 39.6 %whole.1 = bf16[8,8192]{1,0:T(8,128)(2,1)} custom-call(bf16[8,8192]{1,0:T(8,128)(2,1)} %vec_any.1, bf16[3,8192]{1,0:T(4,128)(2,1)} %pts_any.1, s32[1,8192]{1,0:T(1,128)} %perm_any.1, s32[1,256]{1,0:T(1,128)} %bitcast.5, s32[1,256]{1,0:T(1,128)} %bitcast.6, s32[1,256]{1,0:T(1,128)} %bitcast.7, bf16[16,64,512]{2,1,0:T(8,128)(2,1)} %bases_any.1, ...), custom_call_target="tpu_custom_call" | custom-call | tf_op jit(solution)/shard_map/whole/pallas_call | solution.py:502
  39.6 1.6 %copy.13 = bf16[8,8192]{1,0:T(8,128)(2,1)} copy(bf16[8,8192]{1,0:T(8,128)(2,1)} %whole.1) | data formatting | bytes 262144

commit v3 on v0

--- a/solution.py
+++ b/solution.py
@@ -200,12 +200,19 @@
 
 def near_pairs(ext, fa, fb, acc, leaf_len, source, targets, back):
     src = leaf_columns(source, leaf_len)
+    own = None
     for target in targets:
         tgt = leaf_columns(target, leaf_len)
         kernel = lax.rsqrt(tn(fa[:, src], fb[:, tgt])).astype(bf16)
-        acc[:, tgt] += nn(ext[:, src], kernel)
-        if back and target is not source:
-            acc[:, src] += nt(ext[:, tgt], kernel)
+        forward = nn(ext[:, src], kernel)
+        if target is source:
+            own = forward
+        else:
+            acc[:, tgt] += forward
+            if back:
+                own = own + nt(ext[:, tgt], kernel)
+    if back:
+        acc[:, src] += own
 
 
 def finish(
@@ -410,7 +417,7 @@
         near_pairs(vx, fa, fb, acc, leaf_len, leaf, (leaf, leaf + 1, leaf + 2), True)
         return carry
 
-    lax.fori_loop(NEAR, half + NEAR, body, 0)
+    lax.fori_loop(NEAR, half + NEAR, body, 0, unroll=2)
     part = half * leaf_len
     computed = pl.ds(pl.multiple_of(core * part, 128), part)
     to_near = remote(

time: 34.1 us -> 34.1 us (level)
  no operation moved by 1% of the time
where the time goes in v3:
time: 34.1 us; the launch traced here: 34 us
  Pallas kernels  32.4 us (95%)
  local copies, waits for them, and re-layouts  1.57 us (5%)
    pallas_call x1, Pallas kernels, shards(): pl.pallas_call(functools.partial(whole_kernel, peers, leaf_len), out_shap...  32.4 us
    unnamed x1, local copies, waits for them, and re-layouts  1.57 us

profile of v3, /device:TPU:12, one launch (start us, length us, event | category | flops | bytes accessed | tf_op | source)
XLA Modules:
  0.0 34.0 jit_solution(23585192297147288)
XLA Ops:
  0.0 32.4 %whole.1 = bf16[8,8192]{1,0:T(8,128)(2,1)} custom-call(bf16[8,8192]{1,0:T(8,128)(2,1)} %vec_any.1, bf16[3,8192]{1,0:T(4,128)(2,1)} %pts_any.1, s32[1,8192]{1,0:T(1,128)} %perm_any.1, s32[1,256]{1,0:T(1,128)} %bitcast.5, s32[1,256]{1,0:T(1,128)} %bitcast.6, s32[1,256]{1,0:T(1,128)} %bitcast.7, bf16[16,64,512]{2,1,0:T(8,128)(2,1)} %bases_any.1, ...), custom_call_target="tpu_custom_call" | custom-call | tf_op jit(solution)/shard_map/whole/pallas_call | solution.py:483
  32.4 1.6 %copy.13 = bf16[8,8192]{1,0:T(8,128)(2,1)} copy(bf16[8,8192]{1,0:T(8,128)(2,1)} %whole.1) | data formatting | bytes 262144
